TPU v7x, 128 devices: a whole 4x4x4 slice. The times are simulated.
128 devices in a mesh: dp: 32 (over y, z, core), cent: 4 (over x).
Axes of the slice: x: 4, y: 4, z: 4, core: 2. Of those that a mesh axis runs over, the one named last changes fastest.
Arguments:
- embeddings: bfloat16 [32768, 1024], P('dp'), may hold values from -8 to 8, as said below
- centroids: bfloat16 [16384, 1024], P('cent'), may hold values from -0.125 to 0.125, as said below
Outputs:
- log_norm: float32 [32768], P('dp')
- new_centroids: bfloat16 [16384, 1024], P('cent', 'dp')
Inputs may be any that keep to these rules, and one draw needn't show every extreme that they name: Real-valued embeddings. Real-valued centroids.
All inputs are finite; a program needn't handle non-finite values.
Results may differ from a plain program's by a relative error of at most 0.006.
Values may be sent and summed in bfloat16 or wider, within the bound.
A program may use at most 128 MiB of HBM per device.

v0:
```python
import jax
import jax.numpy as jnp
from jax import lax
from jax.sharding import PartitionSpec as P

sharpness = 2.0
pseudo_count = 1.0


def per_device(embeddings, centroids):
    dp_index = lax.axis_index("dp")
    scores = sharpness * jnp.einsum(
        "rd,kd->rk", embeddings, centroids, preferred_element_type=jnp.float32
    )
    row_max = lax.pmax(jnp.max(scores, axis=1), "cent")
    row_total = lax.psum(jnp.sum(jnp.exp(scores - row_max[:, None]), axis=1), "cent")
    log_norm = row_max + jnp.log(row_total)
    resp = jnp.exp(scores - log_norm[:, None]).astype(jnp.bfloat16)
    mass_part = jnp.sum(resp, axis=0, dtype=jnp.float32)
    weighted_part = jnp.einsum("rk,rd->kd", resp, embeddings, preferred_element_type=jnp.float32)
    weighted = lax.psum_scatter(weighted_part, "dp", scatter_dimension=1, tiled=True)
    mass = lax.psum(mass_part, "dp")
    col_count = weighted.shape[1]
    previous = lax.dynamic_slice_in_dim(centroids, dp_index * col_count, col_count, 1)
    updated = (weighted + pseudo_count * previous.astype(jnp.float32)) / (mass + pseudo_count)[
        :, None
    ]
    new_centroids = updated.astype(jnp.bfloat16)
    return (log_norm, new_centroids)


def solution(mesh):
    return jax.shard_map(
        per_device,
        mesh=mesh,
        in_specs=(P("dp", None), P("cent", None)),
        out_specs=(P("dp"), P("cent", "dp")),
        check_vma=False,
    )
```

profile of v0, /device:TPU:2, one launch (start us, length us, event | category | flops | bytes accessed | tf_op | source)
XLA Modules:
  0.0 214.5 jit_solution(9602771233710324116)
XLA Ops:
  7.2 0.0 copy-start
  7.2 0.0 reduce-scatter.2.cloned.1.call-start
  7.2 1.5 copy-done
  8.8 14.6 %multiply_reduce_fusion = (f32[1024]{0:T(1024)S(1)}, f32[1024,4096]{1,0:T(8,128)}) fusion(bf16[1024,1024]{1,0:T(8,128)(2,1)S(1)} %copy-done, bf16[4096,1024]{1,0:T(8,128)(2,1)} %param.3), kind=kOutput, calls=%fused_computation.3 | convolution fusion | flops 8598322176 | bytes 27267072 | tf_op jit(solution)/shard_map/rd,kd->rk/dot_general | solution.py:12
  23.3 8.6 %pmax.7 = f32[1024]{0:T(1024)S(1)} all-reduce(f32[1024]{0:T(1024)S(1)} %get-tuple-element.2), channel_id=1, replica_groups=mesh['dp'=32,'cent'=4] {'cent'}, use_global_device_ids=true, to_apply=%region_1.0 | all-reduce | flops 1024 | bytes 8192 | tf_op jit(solution)/shard_map/pmax | solution.py:15
  31.9 8.6 %exponential_reduce_fusion = f32[1024]{0:T(1024)S(1)} fusion(f32[1024,4096]{1,0:T(8,128)} %get-tuple-element.3, f32[1024]{0:T(1024)S(1)} %pmax.7), kind=kLoop, calls=%fused_computation.2 | loop fusion | flops 12581888 | bytes 16785408 | tf_op jit(solution)/shard_map/reduce_sum | solution.py:16
  40.5 10.1 %psum.14 = f32[1024]{0:T(1024)S(1)} all-reduce(f32[1024]{0:T(1024)S(1)} %exponential_reduce_fusion), channel_id=1, replica_groups=mesh['dp'=32,'cent'=4] {'cent'}, use_global_device_ids=true, to_apply=%region_3.0 | all-reduce | flops 1024 | bytes 8192 | tf_op jit(solution)/shard_map/psum | solution.py:16
  50.7 0.0 copy-start.1
  50.7 16.3 %fusion = f32[4096,1024]{0,1:T(8,128)} fusion(bf16[1024,1024]{1,0:T(8,128)(2,1)S(1)} %copy-done, f32[1024,4096]{1,0:T(8,128)} %get-tuple-element.3, f32[1024]{0:T(1024)S(1)} %log_add_fusion), kind=kOutput, calls=%fused_computation.8 | convolution fusion | flops 8602517504 | bytes 35655680 | tf_op jit(solution)/shard_map/rk,rd->kd/dot_general | solution.py:20
  67.0 0.0 reduce-scatter.2.cloned.1.call-update
  67.0 1.6 constant_dynamic-slice_fusion
  68.6 0.3 copy.5
  68.9 0.0 copy-done.1
  68.9 9.3 %convert_reduce_fusion = f32[4096]{0:T(1024)S(1)} fusion(f32[1024]{0:T(1024)S(1)} %log_add_fusion, f32[1024,4096]{1,0:T(8,128)} %get-tuple-element.3), kind=kLoop, calls=%fused_computation | loop fusion | flops 20967424 | bytes 16797696 | tf_op jit(solution)/shard_map/reduce_sum | solution.py:19
  78.2 127.7 %psum.15 = f32[4096]{0:T(1024)S(1)} all-reduce(f32[4096]{0:T(1024)S(1)} %convert_reduce_fusion), channel_id=1, replica_groups=mesh['dp'=32,'cent'=4] {'dp'}, use_global_device_ids=true, to_apply=%region_6.0 | all-reduce | flops 4096 | bytes 32768 | tf_op jit(solution)/shard_map/psum | solution.py:22
  205.9 0.0 reduce-scatter.2.cloned.1.call-done
  205.9 1.8 divide_convert_fusion
  (2 shorter events, 0.0 us)
Async XLA Ops:
  7.2 1.6 copy-start
  7.2 198.7 %reduce-scatter.2.cloned.1.call-start = ((), (), s32[]{:S(2)}) async-start(), calls=%async_computation.1 | async-start | bytes 17301504 | tf_op jit(solution)/shard_map/reduce_scatter | solution.py:21
  50.7 18.2 %copy-start.1 = (f32[1024]{0:T(1024)}, f32[1024]{0:T(1024)S(1)}, u32[]{:S(2)}) copy-start(f32[1024]{0:T(1024)S(1)} %log_add_fusion) | copy-start | bytes 12292
Sparse Core Ops, SparseCore 0:
  67.1 116.6 reduce-scatter.1
where the time goes:
time: 215 us
  blocking collectives  146 us (68%)
  matrix products  30.8 us (14%)
  other arithmetic  19.7 us (9%)
  between operations  14.1 us (7%)
  local copies, waits for them, and re-layouts  3.45 us (2%)
    psum x1, blocking collectives, per_device(): mass = lax.psum(mass_part, 'dp')  128 us
    dot_general x1, matrix products, per_device(): jnp.einsum('rk,rd->kd', resp, embeddings, preferred_element_type=jnp.floa...  16.3 us
    dot_general x1, matrix products, per_device(): jnp.einsum('rd,kd->rk', embeddings, centroids, preferred_element_type=jnp...  14.6 us
    psum x1, blocking collectives, per_device(): lax.psum(jnp.sum(jnp.exp(scores - row_max[:, None]), axis=1), 'cent')  10.1 us
    reduce_sum x1, other arithmetic, per_device(): mass_part = jnp.sum(resp, axis=0, dtype=jnp.float32)  9.3 us
    reduce_sum x1, other arithmetic, per_device(): jnp.sum(jnp.exp(scores - row_max[:, None]), axis=1)  8.62 us
    pmax x1, blocking collectives, per_device(): row_max = lax.pmax(jnp.max(scores, axis=1), 'cent')  8.59 us
  transfers between devices with their start and end apart: 1, of which 0 were waited for; matrix products, arithmetic and copies ran while one was open for 5% of the time, Pallas kernels for 0%

commit v1 on v0

v1 whole, which is shorter than its diff:
```python
import jax
import jax.numpy as jnp
from jax import lax
from jax.experimental import pallas as pl
from jax.experimental.pallas import tpu as pltpu
from jax.sharding import PartitionSpec as P

MESH = pl.DeviceIdType.MESH
F32, BF16 = jnp.float32, jnp.bfloat16

SIDE = 4
D = 1024
ROWS = 1024
CENT = 4096
HALF = CENT // 2
BLOCK = 256
CHUNK = 256
N_BLOCKS = 2 * ROWS // BLOCK
N_CHUNKS = HALF // CHUNK
CHIP_COLS = D // (SIDE * SIDE)
DEV_COLS = CHIP_COLS // 2

OTHERS = [(d, c) for c in range(2) for d in range(SIDE) if (d, c) != (0, 0)]


def kernel(
    e_hbm, c_hbm, norm_ref, out_ref,
    emb, emb2, emb_t, cent, scores, resp, weighted, relay, gather_a, gather_b, second, gather_c, previous,
    lse, lse_in, norm_row, mass, mass_in, mass_y, mass_in2, den,
    load_sem, emb_send, emb_recv, lse_send, lse_recv, a_send, a_recv, b_send, b_recv, c_send, c_recv,
    mass_send, mass_recv,
):
    dp = lax.axis_index("dp")
    x = lax.axis_index("cent")
    y, z, core = dp // 8, lax.rem(dp // 2, SIDE), lax.rem(dp, 2)

    def device(dx, dy, dz, dc):
        return {
            "dp": (lax.rem(y + dy, SIDE) * SIDE + lax.rem(z + dz, SIDE)) * 2 + lax.rem(core + dc, 2),
            "cent": lax.rem(x + dx, SIDE),
        }

    def along(axis, d, dc):
        return device(*[d if a == axis else 0 for a in range(3)], dc)

    def send(src, dst, send_sem, recv_sem, target):
        pltpu.make_async_remote_copy(
            src_ref=src, dst_ref=dst, send_sem=send_sem, recv_sem=recv_sem, device_id=target, device_id_type=MESH
        ).start()

    def wait(ref, sem):
        pltpu.make_async_copy(ref, ref, sem).wait()

    e_loads = [
        pltpu.make_async_copy(e_hbm.at[pl.ds(b * BLOCK, BLOCK)], emb.at[0, pl.ds(b * BLOCK, BLOCK)], load_sem.at[b])
        for b in range(4)
    ]
    c_loads = [
        pltpu.make_async_copy(
            c_hbm.at[pl.ds(core * HALF + m * 512, 512)], cent.at[0, pl.ds(m * 512, 512)], load_sem.at[4 + m]
        )
        for m in range(4)
    ]
    c_other = pltpu.make_async_copy(c_hbm.at[pl.ds((1 - core) * HALF, HALF)], cent.at[1], load_sem.at[8])
    for copy in [e_loads[0], *c_loads, *e_loads[1:], c_other]:
        copy.start()

    barrier = pltpu.get_barrier_semaphore()
    for d, dc in OTHERS:
        for axis in range(3):
            if d or axis == 0:
                pl.semaphore_signal(barrier, inc=1, device_id=along(axis, d, dc), device_id_type=MESH)

    def statistics(b):
        ref = scores.at[b]
        top = ref[0:64].reshape(8, 8, BLOCK).max(0)
        for j in range(64, HALF, 64):
            top = jnp.maximum(top, ref[j : j + 64].reshape(8, 8, BLOCK).max(0))
        top = jnp.max(top, axis=0, keepdims=True)
        total = jnp.zeros((8, BLOCK), F32)
        for j in range(0, HALF, 64):
            total = total + jnp.exp(ref[j : j + 64] - top).reshape(8, 8, BLOCK).sum(0)
        value = top + jnp.log(jnp.sum(total, axis=0, keepdims=True))
        group, row = b // 4, 2 * (b % 4)
        lse[group, row : row + 1] = value[:, 0:128]
        lse[group, row + 1 : row + 2] = value[:, 128:256]

    def send_lse(group):
        for j, (d, dc) in enumerate(OTHERS):
            send(lse.at[group], lse_in.at[group ^ dc, j], lse_send, lse_recv.at[group ^ dc], along(0, d, dc))

    emb_t[D : D + 16, :] = jnp.ones((16, 2 * ROWS), BF16)
    for b in range(N_BLOCKS):
        slot, first = b // 4, (b % 4) * BLOCK
        if b < 3:
            e_loads[b].wait()
        elif b >= 4 and b % 2 == 0:
            wait(emb.at[1, pl.ds(first, 512)], emb_recv.at[b // 2 - 2])
        rows = emb[slot, first : first + BLOCK]
        emb2[...] = rows * BF16(2)
        for m in range(HALF // 512):
            if b == 0:
                c_loads[m].wait()
            scores[b, m * 512 : m * 512 + 512] = lax.dot_general(
                cent[0, m * 512 : m * 512 + 512], emb2[...], (((1,), (1,)), ((), ())), preferred_element_type=F32
            )
        emb_t[0:D, b * BLOCK : (b + 1) * BLOCK] = rows.T
        if b:
            statistics(b - 1)
        if b == 2:
            e_loads[3].wait()
            pl.semaphore_wait(barrier, 19)
            for h in range(2):
                part = pl.ds(h * 512, 512)
                send(emb.at[0, part], emb.at[1, part], emb_send, emb_recv.at[h], device(0, 0, 0, 1))
        if b == 4:
            send_lse(0)
    statistics(N_BLOCKS - 1)
    send_lse(1)

    for group in range(2):
        wait(lse_in.at[group], lse_recv.at[group])
        parts = [lse[group]] + [lse_in[group, j] for j in range(7)]
        top = parts[0]
        for part in parts[1:]:
            top = jnp.maximum(top, part)
        total = jnp.zeros_like(top)
        for part in parts:
            total = total + jnp.exp(part - top)
        norm = top + jnp.log(total)
        if group == 0:
            norm_ref[...] = norm
        for j in range(8):
            at = group * ROWS + j * 128
            norm_row[0:1, at : at + 128] = norm[j : j + 1]

    def exponentials(i):
        for b in range(N_BLOCKS):
            norm = norm_row[0:1, b * BLOCK : (b + 1) * BLOCK]
            for j in range(0, CHUNK, 32):
                at = i * CHUNK + j
                resp[i % 2, j : j + 32, b * BLOCK : (b + 1) * BLOCK] = jnp.exp(
                    scores[b, at : at + 32] - norm
                ).astype(BF16)

    def product(i):
        sums = lax.dot_general(
            emb_t[...], resp[i % 2], (((1,), (1,)), ((), ())), preferred_element_type=F32
        )
        for yy in range(SIDE):
            for zz in range(SIDE):
                at = (yy * SIDE + zz) * CHIP_COLS
                value = sums[at : at + CHIP_COLS].astype(BF16)
                if i % 2 == 0:
                    weighted[i, yy, zz] = value
                else:
                    weighted[i, zz, yy] = value
        mass[2 * i : 2 * i + 1] = sums[D : D + 1, 0:128]
        mass[2 * i + 1 : 2 * i + 2] = sums[D : D + 1, 128:256]

    def places(i):
        return (1, y, 2, z) if i % 2 == 0 else (2, z, 1, y)

    def send_a(i):
        axis, p, _, _ = places(i)
        up, down, far = lax.rem(p + 1, SIDE), lax.rem(p + 3, SIDE), lax.rem(p + 2, SIDE)
        to_up, to_down = along(axis, 1, 0), along(axis, 3, 0)
        lo, hi = pl.ds(0, 2), pl.ds(2, 2)
        send(weighted.at[i, far, lo], gather_a.at[i, 0, 0], a_send, a_recv.at[i, 0], to_up)
        send(weighted.at[i, far, hi], gather_a.at[i, 0, 1], a_send, a_recv.at[i, 0], to_down)
        send(weighted.at[i, up, hi], gather_a.at[i, 1, 0], a_send, a_recv.at[i, 1], to_up)
        send(weighted.at[i, down, lo], gather_a.at[i, 1, 1], a_send, a_recv.at[i, 1], to_down)

    def send_b(i):
        axis, p, _, _ = places(i)
        up, down = lax.rem(p + 1, SIDE), lax.rem(p + 3, SIDE)
        wait(gather_a.at[i, 0], a_recv.at[i, 0])
        relay[i, 0] = (weighted[i, up, 0:2].astype(F32) + gather_a[i, 0, 0].astype(F32)).astype(BF16)
        relay[i, 1] = (weighted[i, down, 2:4].astype(F32) + gather_a[i, 0, 1].astype(F32)).astype(BF16)
        send(relay.at[i, 0], gather_b.at[i, 0], b_send, b_recv.at[i], along(axis, 1, 0))
        send(relay.at[i, 1], gather_b.at[i, 1], b_send, b_recv.at[i], along(axis, 3, 0))

    def send_c(i):
        _, p, axis, q = places(i)
        wait(gather_a.at[i, 1], a_recv.at[i, 1])
        wait(gather_b.at[i], b_recv.at[i])
        low = weighted[i, p, 0:2].astype(F32) + gather_b[i, 0].astype(F32) + gather_a[i, 1, 1].astype(F32)
        high = weighted[i, p, 2:4].astype(F32) + gather_b[i, 1].astype(F32) + gather_a[i, 1, 0].astype(F32)
        second[i, 0:2] = low.astype(BF16).reshape(2, 2, DEV_COLS, CHUNK)
        second[i, 2:4] = high.astype(BF16).reshape(2, 2, DEV_COLS, CHUNK)
        for j, (d, dc) in enumerate(OTHERS):
            send(
                second.at[i, lax.rem(q + d, SIDE), lax.rem(core + dc, 2)], gather_c.at[i, j],
                c_send, c_recv.at[i], along(axis, d, dc),
            )

    def finish(i):
        _, _, _, q = places(i)
        wait(gather_c.at[i], c_recv.at[i])
        at = slice(i * CHUNK, (i + 1) * CHUNK)
        for h in range(2):
            if h == 0:
                total = second[i, q, core].astype(F32)
                for j in range(3):
                    total = total + gather_c[i, j].astype(F32)
            else:
                total = gather_c[i, 3].astype(F32)
                for j in range(4, 7):
                    total = total + gather_c[i, j].astype(F32)
            total = total + previous[h, :, at]
            for k in range(2):
                part = slice(k * 128, (k + 1) * 128)
                out_ref[lax.rem(core + h, 2), :, i * CHUNK + k * 128 : i * CHUNK + (k + 1) * 128] = (
                    total[:, part] / den[h, 2 * i + k : 2 * i + k + 1]
                ).astype(BF16)

    exponentials(0)
    for i in range(N_CHUNKS):
        product(i)
        if i + 1 < N_CHUNKS:
            exponentials(i + 1)
        send_a(i)

    for d in range(1, SIDE):
        send(mass, mass_in.at[d - 1], mass_send, mass_recv.at[0], along(1, d, 0))

    c_other.wait()
    row = lax.broadcasted_iota(jnp.int32, (DEV_COLS, D), 0)
    col = lax.broadcasted_iota(jnp.int32, (DEV_COLS, D), 1)
    pick = jnp.where(col == row + dp * DEV_COLS, 1.0, 0.0).astype(BF16)
    for h in range(2):
        for m in range(0, HALF, 512):
            previous[h, :, m : m + 512] = lax.dot_general(
                pick, cent[h, m : m + 512], (((1,), (1,)), ((), ())), preferred_element_type=F32
            )

    for i in range(4):
        send_b(i)
    wait(mass_in, mass_recv.at[0])
    mass_y[...] = mass[...] + mass_in[0] + mass_in[1] + mass_in[2]
    for j, (d, dc) in enumerate(OTHERS):
        send(mass_y, mass_in2.at[j], mass_send, mass_recv.at[1], along(2, d, dc))
    for i in range(4):
        send_b(i + 4)
        send_c(i)
    wait(mass_in2, mass_recv.at[1])
    den[0] = mass_y[...] + mass_in2[0] + mass_in2[1] + mass_in2[2] + 1.0
    den[1] = mass_in2[3] + mass_in2[4] + mass_in2[5] + mass_in2[6] + 1.0
    for i in range(4):
        send_c(i + 4)
        finish(i)
    wait(emb.at[1], emb_send)
    wait(lse_in, lse_send)
    wait(gather_a, a_send)
    wait(gather_b, b_send)
    wait(mass_in, mass_send)
    wait(mass_in2, mass_send)
    wait(gather_c, c_send)
    for i in range(4, N_CHUNKS):
        finish(i)


def per_device(embeddings, centroids):
    dma = pltpu.SemaphoreType.DMA
    norm, out = pl.pallas_call(
        kernel,
        out_shape=(
            jax.ShapeDtypeStruct((8, 128), F32),
            jax.ShapeDtypeStruct((2, DEV_COLS, HALF), BF16),
        ),
        in_specs=[pl.BlockSpec(memory_space=pl.ANY)] * 2,
        out_specs=(pl.BlockSpec(memory_space=pltpu.VMEM),) * 2,
        scratch_shapes=[
            pltpu.VMEM((2, ROWS, D), BF16),
            pltpu.VMEM((BLOCK, D), BF16),
            pltpu.VMEM((D + 16, 2 * ROWS), BF16),
            pltpu.VMEM((2, HALF, D), BF16),
            pltpu.VMEM((N_BLOCKS, HALF, BLOCK), F32),
            pltpu.VMEM((2, CHUNK, 2 * ROWS), BF16),
            pltpu.VMEM((N_CHUNKS, SIDE, SIDE, CHIP_COLS, CHUNK), BF16),
            pltpu.VMEM((N_CHUNKS, 2, 2, CHIP_COLS, CHUNK), BF16),
            pltpu.VMEM((N_CHUNKS, 2, 2, 2, CHIP_COLS, CHUNK), BF16),
            pltpu.VMEM((N_CHUNKS, 2, 2, CHIP_COLS, CHUNK), BF16),
            pltpu.VMEM((N_CHUNKS, SIDE, 2, DEV_COLS, CHUNK), BF16),
            pltpu.VMEM((N_CHUNKS, 7, DEV_COLS, CHUNK), BF16),
            pltpu.VMEM((2, DEV_COLS, HALF), F32),
            pltpu.VMEM((2, 8, 128), F32),
            pltpu.VMEM((2, 7, 8, 128), F32),
            pltpu.VMEM((1, 2 * ROWS), F32),
            pltpu.VMEM((16, 128), F32),
            pltpu.VMEM((3, 16, 128), F32),
            pltpu.VMEM((16, 128), F32),
            pltpu.VMEM((7, 16, 128), F32),
            pltpu.VMEM((2, 16, 128), F32),
            dma((9,)),
            dma, dma((2,)),
            dma, dma((2,)),
            dma, dma((N_CHUNKS, 2)),
            dma, dma((N_CHUNKS,)),
            dma, dma((N_CHUNKS,)),
            dma, dma((2,)),
        ],
        compiler_params=pltpu.CompilerParams(
            collective_id=0, has_side_effects=True, vmem_limit_bytes=60 * 2**20
        ),
    )(embeddings, centroids)
    return norm.reshape(ROWS), out.transpose(0, 2, 1).reshape(CENT, DEV_COLS)


def solution(mesh):
    return jax.shard_map(
        per_device,
        mesh=mesh,
        in_specs=(P("dp", None), P("cent", None)),
        out_specs=(P("dp"), P("cent", "dp")),
        check_vma=False,
    )
```

time: 215 us -> 61.6 us (0.29)
  the two profiles are of different devices: /device:TPU:2 before, /device:TPU:1 now
where the time goes in v1:
time: 61.6 us; the launch traced here: 61.4 us
  Pallas kernels  57.8 us (94%)
  local copies, waits for them, and re-layouts  2.95 us (5%)
  between operations  0.64 us (1%)
    pallas_call x1, Pallas kernels, per_device(): pl.pallas_call(kernel, out_shape=(jax.ShapeDtypeStruct((8, 128), F32), ja...  57.8 us
    reshape x1, local copies, waits for them, and re-layouts, per_device(): return (norm.reshape(ROWS), out.transpose(0, 2, 1).reshape(CENT, DEV_COLS))  1.67 us
    unnamed x1, local copies, waits for them, and re-layouts  1.28 us

profile of v1, /device:TPU:1, one launch (start us, length us, event | category | flops | bytes accessed | tf_op | source)
XLA Modules:
  0.0 61.4 jit_solution(6645413001506471777)
XLA Ops:
  0.6 57.8 %shard_map.41 = (f32[8,128]{1,0:T(8,128)}, bf16[2,32,2048]{2,1,0:T(8,128)(2,1)}) custom-call(bf16[1024,1024]{1,0:T(8,128)(2,1)} %e_hbm.1, bf16[4096,1024]{1,0:T(8,128)(2,1)} %c_hbm.1), custom_call_target="tpu_custom_call" | custom-call | tf_op jit(solution)/shard_map/pallas_call | solution.py:265
  58.5 1.7 %copy.5 = bf16[2,4,8,2048]{3,2,0,1:T(8,128)(2,1)} copy(bf16[2,4,8,2048]{3,2,1,0:T(8,128)(2,1)} %bitcast.5) | data formatting | bytes 524288 | tf_op jit(solution)/shard_map/reshape | solution.py:307
  60.1 1.3 %copy.7 = f32[1024]{0:T(1024)} copy(f32[1024]{0:T(1024)} %bitcast.6) | data formatting | bytes 8192

commit v2 on v1

v2 whole, which is shorter than its diff:
```python
import jax
import jax.numpy as jnp
from jax import lax
from jax.experimental import pallas as pl
from jax.experimental.pallas import tpu as pltpu
from jax.sharding import PartitionSpec as P

MESH = pl.DeviceIdType.MESH
F32, BF16 = jnp.float32, jnp.bfloat16

SIDE = 4
D = 1024
ROWS = 1024
CENT = 4096
HALF = CENT // 2
BLOCK = 256
TILE = 256
CHUNK = 256
N_BLOCKS = 2 * ROWS // BLOCK
N_CHUNKS = HALF // CHUNK
CHIP_COLS = D // (SIDE * SIDE)
DEV_COLS = CHIP_COLS // 2

OTHERS = [(d, c) for c in range(2) for d in range(SIDE) if (d, c) != (0, 0)]


def kernel(
    e_hbm, c_hbm, norm_ref, out_ref,
    emb, emb2, emb_t, cent, scores, resp, weighted, relay, gather_a, gather_b, second, gather_c, previous,
    lse, lse_in, norm_row, mass, mass_in, mass_y, mass_in2, den,
    load_sem, emb_send, emb_recv, lse_send, lse_recv, a_send, a_recv, b_send, b_recv, c_send, c_recv,
    mass_send, mass_recv,
):
    dp = lax.axis_index("dp")
    x = lax.axis_index("cent")
    y, z, core = dp // 8, lax.rem(dp // 2, SIDE), lax.rem(dp, 2)

    def device(dx, dy, dz, dc):
        return {
            "dp": (lax.rem(y + dy, SIDE) * SIDE + lax.rem(z + dz, SIDE)) * 2 + lax.rem(core + dc, 2),
            "cent": lax.rem(x + dx, SIDE),
        }

    def along(axis, d, dc):
        return device(*[d if a == axis else 0 for a in range(3)], dc)

    def send(src, dst, send_sem, recv_sem, target):
        pltpu.make_async_remote_copy(
            src_ref=src, dst_ref=dst, send_sem=send_sem, recv_sem=recv_sem, device_id=target, device_id_type=MESH
        ).start()

    def wait(ref, sem):
        pltpu.make_async_copy(ref, ref, sem).wait()

    loads = [
        pltpu.make_async_copy(e_hbm, emb.at[pl.ds(0, ROWS)], load_sem.at[0]),
        pltpu.make_async_copy(c_hbm.at[pl.ds(core * HALF, HALF)], cent.at[0], load_sem.at[1]),
    ]
    for copy in loads:
        copy.start()
    c_other = pltpu.make_async_copy(c_hbm.at[pl.ds((1 - core) * HALF, HALF)], cent.at[1], load_sem.at[2])

    barrier = pltpu.get_barrier_semaphore()
    for d, dc in OTHERS:
        for axis in range(3):
            if d or axis == 0:
                pl.semaphore_signal(barrier, inc=1, device_id=along(axis, d, dc), device_id_type=MESH)

    def statistics(tile, top, total):
        for j in range(0, TILE, 64):
            part = tile[j : j + 64].reshape(8, 8, BLOCK)
            high = part.max(0)
            if top is None:
                total = jnp.exp(part - high[None]).sum(0)
            else:
                high = jnp.maximum(top, high)
                total = total * jnp.exp(top - high) + jnp.exp(part - high[None]).sum(0)
            top = high
        return top, total

    def row_lse(b, top, total):
        high = jnp.max(top, axis=0, keepdims=True)
        value = high + jnp.log(jnp.sum(total * jnp.exp(top - high), axis=0, keepdims=True))
        lse[b // 4, pl.ds(2 * lax.rem(b, 4), 1)] = value[:, 0:128]
        lse[b // 4, pl.ds(2 * lax.rem(b, 4) + 1, 1)] = value[:, 128:256]

    def send_lse(group):
        for j, (d, dc) in enumerate(OTHERS):
            send(lse.at[group], lse_in.at[group ^ dc, j], lse_send, lse_recv.at[group ^ dc], along(0, d, dc))

    def send_emb():
        for h in range(2):
            part = pl.ds(h * 512, 512)
            send(emb.at[part], emb.at[pl.ds(ROWS + h * 512, 512)], emb_send, emb_recv.at[h], device(0, 0, 0, 1))

    def norms(group):
        wait(lse_in.at[group], lse_recv.at[group])
        parts = [lse[group]] + [lse_in[group, j] for j in range(7)]
        top = parts[0]
        for part in parts[1:]:
            top = jnp.maximum(top, part)
        total = jnp.zeros_like(top)
        for part in parts:
            total = total + jnp.exp(part - top)
        norm = top + jnp.log(total)
        if group == 0:
            norm_ref[...] = norm
        for j in range(8):
            at = group * ROWS + j * 128
            norm_row[0:1, at : at + 128] = norm[j : j + 1]

    def take_previous(m, carry):
        at = pl.multiple_of((m % N_CHUNKS) * CHUNK, CHUNK)
        columns = pl.ds(pl.multiple_of(dp // 4 * 128, 128), 128)
        previous[m // N_CHUNKS, m % N_CHUNKS] = cent[m // N_CHUNKS, pl.ds(at, CHUNK), columns].T
        return carry

    def score_block(b):
        at = pl.multiple_of(b * BLOCK, BLOCK)
        rows = emb[pl.ds(at, BLOCK)]
        emb2[...] = rows * BF16(2)
        top = total = None
        for m in range(HALF // TILE):
            tile = lax.dot_general(
                cent[0, m * TILE : (m + 1) * TILE], emb2[...], (((1,), (1,)), ((), ())), preferred_element_type=F32
            )
            scores[b, m * TILE : (m + 1) * TILE] = tile
            top, total = statistics(tile, top, total)
        row_lse(b, top, total)
        emb_t[0:D, pl.ds(at, BLOCK)] = rows.T

    def score_step(q, carry):
        @pl.when(q == 1)
        def _():
            c_other.start()
            pl.semaphore_wait(barrier, 19)
            send_emb()

        for h in range(2):

            @pl.when(q == 2 + h)
            def _():
                wait(emb.at[pl.ds(ROWS + h * 512, 512)], emb_recv.at[h])

        for b in range(2):
            score_block(2 * q + b)

        @pl.when(q == 1)
        def _():
            send_lse(0)

        return carry

    emb_t[D : D + 16, :] = jnp.ones((16, 2 * ROWS), BF16)
    for copy in loads:
        copy.wait()
    lax.fori_loop(0, 4, score_step, 0)
    send_lse(1)
    c_other.wait()
    lax.fori_loop(0, 2 * N_CHUNKS, take_previous, 0)
    norms(0)
    norms(1)

    def exponentials(i, slot):
        for b in range(N_BLOCKS):
            norm = norm_row[0:1, b * BLOCK : (b + 1) * BLOCK]
            for j in range(0, CHUNK, 32):
                at = pl.multiple_of(i * CHUNK + j, 32)
                resp[slot, j : j + 32, b * BLOCK : (b + 1) * BLOCK] = jnp.exp(
                    scores[b, pl.ds(at, 32)] - norm
                ).astype(BF16)

    def product(i, slot):
        sums = lax.dot_general(
            emb_t[...], resp[slot], (((1,), (1,)), ((), ())), preferred_element_type=F32
        )
        for yy in range(SIDE):
            for zz in range(SIDE):
                at = (yy * SIDE + zz) * CHIP_COLS
                value = sums[at : at + CHIP_COLS].astype(BF16)
                if slot == 0:
                    weighted[i, yy, zz] = value
                else:
                    weighted[i, zz, yy] = value
        for k in range(2):
            mass[pl.ds(2 * i + k, 1)] = sums[D : D + 1, k * 128 : (k + 1) * 128]

    def places(slot):
        return (1, y, 2, z) if slot == 0 else (2, z, 1, y)

    def send_a(i, slot):
        axis, p, _, _ = places(slot)
        up, down, far = lax.rem(p + 1, SIDE), lax.rem(p + 3, SIDE), lax.rem(p + 2, SIDE)
        to_up, to_down = along(axis, 1, 0), along(axis, 3, 0)
        lo, hi = pl.ds(0, 2), pl.ds(2, 2)
        send(weighted.at[i, far, lo], gather_a.at[i, 0, 0], a_send, a_recv.at[i, 0], to_up)
        send(weighted.at[i, far, hi], gather_a.at[i, 0, 1], a_send, a_recv.at[i, 0], to_down)
        send(weighted.at[i, up, hi], gather_a.at[i, 1, 0], a_send, a_recv.at[i, 1], to_up)
        send(weighted.at[i, down, lo], gather_a.at[i, 1, 1], a_send, a_recv.at[i, 1], to_down)

    def relay_sums(i, slot):
        _, p, _, _ = places(slot)
        up, down = lax.rem(p + 1, SIDE), lax.rem(p + 3, SIDE)
        wait(gather_a.at[i, 0], a_recv.at[i, 0])
        relay[i, 0] = (weighted[i, up, 0:2].astype(F32) + gather_a[i, 0, 0].astype(F32)).astype(BF16)
        relay[i, 1] = (weighted[i, down, 2:4].astype(F32) + gather_a[i, 0, 1].astype(F32)).astype(BF16)

    def send_b(i, slot):
        axis, _, _, _ = places(slot)
        send(relay.at[i, 0], gather_b.at[i, 0], b_send, b_recv.at[i], along(axis, 1, 0))
        send(relay.at[i, 1], gather_b.at[i, 1], b_send, b_recv.at[i], along(axis, 3, 0))

    def second_sums(i, slot):
        _, p, _, _ = places(slot)
        wait(gather_a.at[i, 1], a_recv.at[i, 1])
        wait(gather_b.at[i], b_recv.at[i])
        low = weighted[i, p, 0:2].astype(F32) + gather_b[i, 0].astype(F32) + gather_a[i, 1, 1].astype(F32)
        high = weighted[i, p, 2:4].astype(F32) + gather_b[i, 1].astype(F32) + gather_a[i, 1, 0].astype(F32)
        second[i, 0:2] = low.astype(BF16).reshape(2, 2, DEV_COLS, CHUNK)
        second[i, 2:4] = high.astype(BF16).reshape(2, 2, DEV_COLS, CHUNK)

    def send_c(i, slot):
        _, _, axis, q = places(slot)
        for j, (d, dc) in enumerate(OTHERS):
            send(
                second.at[i, lax.rem(q + d, SIDE), lax.rem(core + dc, 2)], gather_c.at[i, j],
                c_send, c_recv.at[i], along(axis, d, dc),
            )

    def finish(i, slot):
        _, _, _, q = places(slot)
        wait(gather_c.at[i], c_recv.at[i])
        own = pl.ds(pl.multiple_of(lax.rem(dp, 4) * DEV_COLS, DEV_COLS), DEV_COLS)
        for h in range(2):
            if h == 0:
                total = second[i, q, core].astype(F32)
                for j in range(3):
                    total = total + gather_c[i, j].astype(F32)
            else:
                total = gather_c[i, 3].astype(F32)
                for j in range(4, 7):
                    total = total + gather_c[i, j].astype(F32)
            total = total + previous[h, i, own].astype(F32)
            for k in range(2):
                part = slice(k * 128, (k + 1) * 128)
                at = pl.multiple_of(lax.rem(core + h, 2) * HALF + i * CHUNK + k * 128, 128)
                out_ref[:, pl.ds(at, 128)] = (
                    total[:, part] / den[h, pl.ds(2 * i + k, 1)]
                ).astype(BF16)

    def send_mass(stage):
        if stage == 0:
            for d in range(1, SIDE):
                send(mass, mass_in.at[d - 1], mass_send, mass_recv.at[0], along(1, d, 0))
        elif stage == 1:
            wait(mass_in, mass_recv.at[0])
            mass_y[...] = mass[...] + mass_in[0] + mass_in[1] + mass_in[2]
            for j, (d, dc) in enumerate(OTHERS):
                send(mass_y, mass_in2.at[j], mass_send, mass_recv.at[1], along(2, d, dc))
        else:
            wait(mass_in2, mass_recv.at[1])
            den[0] = mass_y[...] + mass_in2[0] + mass_in2[1] + mass_in2[2] + 1.0
            den[1] = mass_in2[3] + mass_in2[4] + mass_in2[5] + mass_in2[6] + 1.0

    def sums_step(j, carry):
        product(2 * j, 0)
        exponentials(2 * j + 1, 1)
        product(2 * j + 1, 1)
        exponentials(jnp.minimum(2 * j + 2, N_CHUNKS - 1), 0)
        send_a(2 * j, 0)
        send_a(2 * j + 1, 1)
        return carry

    def pair(*steps):
        def both(j, carry):
            for step in steps:
                step(2 * j, 0)
                step(2 * j + 1, 1)
            return carry

        lax.fori_loop(0, N_CHUNKS // 2, both, 0)

    exponentials(0, 0)
    lax.fori_loop(0, N_CHUNKS // 2, sums_step, 0)
    send_mass(0)
    pair(relay_sums, send_b)
    send_mass(1)
    pair(second_sums, send_c)
    send_mass(2)
    pair(finish)
    wait(emb.at[pl.ds(ROWS, ROWS)], emb_send)
    wait(lse_in, lse_send)
    wait(gather_a, a_send)
    wait(gather_b, b_send)
    wait(mass_in, mass_send)
    wait(mass_in2, mass_send)
    wait(gather_c, c_send)


def per_device(embeddings, centroids):
    dma = pltpu.SemaphoreType.DMA
    norm, out = pl.pallas_call(
        kernel,
        out_shape=(
            jax.ShapeDtypeStruct((8, 128), F32),
            jax.ShapeDtypeStruct((DEV_COLS, CENT), BF16),
        ),
        in_specs=[pl.BlockSpec(memory_space=pl.ANY)] * 2,
        out_specs=(pl.BlockSpec(memory_space=pltpu.VMEM),) * 2,
        scratch_shapes=[
            pltpu.VMEM((2 * ROWS, D), BF16),
            pltpu.VMEM((BLOCK, D), BF16),
            pltpu.VMEM((D + 16, 2 * ROWS), BF16),
            pltpu.VMEM((2, HALF, D), BF16),
            pltpu.VMEM((N_BLOCKS, HALF, BLOCK), F32),
            pltpu.VMEM((2, CHUNK, 2 * ROWS), BF16),
            pltpu.VMEM((N_CHUNKS, SIDE, SIDE, CHIP_COLS, CHUNK), BF16),
            pltpu.VMEM((N_CHUNKS, 2, 2, CHIP_COLS, CHUNK), BF16),
            pltpu.VMEM((N_CHUNKS, 2, 2, 2, CHIP_COLS, CHUNK), BF16),
            pltpu.VMEM((N_CHUNKS, 2, 2, CHIP_COLS, CHUNK), BF16),
            pltpu.VMEM((N_CHUNKS, SIDE, 2, DEV_COLS, CHUNK), BF16),
            pltpu.VMEM((N_CHUNKS, 7, DEV_COLS, CHUNK), BF16),
            pltpu.VMEM((2, N_CHUNKS, 128, CHUNK), BF16),
            pltpu.VMEM((2, 8, 128), F32),
            pltpu.VMEM((2, 7, 8, 128), F32),
            pltpu.VMEM((1, 2 * ROWS), F32),
            pltpu.VMEM((16, 128), F32),
            pltpu.VMEM((3, 16, 128), F32),
            pltpu.VMEM((16, 128), F32),
            pltpu.VMEM((7, 16, 128), F32),
            pltpu.VMEM((2, 16, 128), F32),
            dma((3,)),
            dma, dma((2,)),
            dma, dma((2,)),
            dma, dma((N_CHUNKS, 2)),
            dma, dma((N_CHUNKS,)),
            dma, dma((N_CHUNKS,)),
            dma, dma((2,)),
        ],
        compiler_params=pltpu.CompilerParams(
            collective_id=0, has_side_effects=True, vmem_limit_bytes=60 * 2**20
        ),
    )(embeddings, centroids)
    return norm.reshape(ROWS), out.T


def solution(mesh):
    return jax.shard_map(
        per_device,
        mesh=mesh,
        in_specs=(P("dp", None), P("cent", None)),
        out_specs=(P("dp"), P("cent", "dp")),
        check_vma=False,
    )
```

time: 61.6 us -> 55.1 us (0.89)
  Pallas kernels: 57.8 us -> 51.3 us
    pallas_call x1, Pallas kernels: 57.8 us -> 51.3 us  [per_device(): pl.pallas_call(kernel, out_shape=(jax.ShapeDtypeStruct((8, 128), F32), ja...]
    reshape x1 -> x0, local copies, waits for them, and re-layouts: 1.67 us -> none  [per_device(): return (norm.reshape(ROWS), out.transpose(0, 2, 1).reshape(CENT, DEV_COLS))]
    unnamed x1 -> x2, local copies, waits for them, and re-layouts: 1.28 us -> 2.95 us
where the time goes in v2:
time: 55.1 us; the launch traced here: 54.9 us
  Pallas kernels  51.3 us (93%)
  local copies, waits for them, and re-layouts  2.95 us (5%)
  between operations  0.64 us (1%)
    pallas_call x1, Pallas kernels, per_device(): pl.pallas_call(kernel, out_shape=(jax.ShapeDtypeStruct((8, 128), F32), ja...  51.3 us
    unnamed x2, local copies, waits for them, and re-layouts  2.95 us

profile of v2, /device:TPU:1, one launch (start us, length us, event | category | flops | bytes accessed | tf_op | source)
XLA Modules:
  0.0 54.9 jit_solution(14377712632847347875)
XLA Ops:
  0.6 51.3 %shard_map.41 = (f32[8,128]{1,0:T(8,128)}, bf16[32,4096]{1,0:T(8,128)(2,1)}) custom-call(bf16[1024,1024]{1,0:T(8,128)(2,1)} %e_hbm.1, bf16[4096,1024]{1,0:T(8,128)(2,1)} %c_hbm.1), custom_call_target="tpu_custom_call" | custom-call | tf_op jit(solution)/shard_map/pallas_call | solution.py:302
  52.0 1.3 %copy.6 = f32[1024]{0:T(1024)} copy(f32[1024]{0:T(1024)} %bitcast.3) | data formatting | bytes 8192
  53.2 1.7 %copy.7 = bf16[4096,32]{0,1:T(8,128)(2,1)} copy(bf16[4096,32]{0,1:T(8,128)(2,1)} %bitcast.2) | data formatting | bytes 524288

commit v3 on v2

--- a/solution.py
+++ b/solution.py
@@ -22,6 +22,7 @@
 DEV_COLS = CHIP_COLS // 2
 
 OTHERS = [(d, c) for c in range(2) for d in range(SIDE) if (d, c) != (0, 0)]
+FAR_FIRST = (1, 5, 0, 2, 4, 6, 3)
 
 
 def kernel(
@@ -53,8 +54,9 @@
         pltpu.make_async_copy(ref, ref, sem).wait()
 
     loads = [
-        pltpu.make_async_copy(e_hbm, emb.at[pl.ds(0, ROWS)], load_sem.at[0]),
+        pltpu.make_async_copy(e_hbm.at[pl.ds(0, 512)], emb.at[pl.ds(0, 512)], load_sem.at[0]),
         pltpu.make_async_copy(c_hbm.at[pl.ds(core * HALF, HALF)], cent.at[0], load_sem.at[1]),
+        pltpu.make_async_copy(e_hbm.at[pl.ds(512, 512)], emb.at[pl.ds(512, 512)], load_sem.at[3]),
     ]
     for copy in loads:
         copy.start()
@@ -85,7 +87,8 @@
         lse[b // 4, pl.ds(2 * lax.rem(b, 4) + 1, 1)] = value[:, 128:256]
 
     def send_lse(group):
-        for j, (d, dc) in enumerate(OTHERS):
+        for j in FAR_FIRST:
+            d, dc = OTHERS[j]
             send(lse.at[group], lse_in.at[group ^ dc, j], lse_send, lse_recv.at[group ^ dc], along(0, d, dc))
 
     def send_emb():
@@ -132,6 +135,7 @@
     def score_step(q, carry):
         @pl.when(q == 1)
         def _():
+            loads[2].wait()
             c_other.start()
             pl.semaphore_wait(barrier, 19)
             send_emb()
@@ -152,7 +156,7 @@
         return carry
 
     emb_t[D : D + 16, :] = jnp.ones((16, 2 * ROWS), BF16)
-    for copy in loads:
+    for copy in loads[:2]:
         copy.wait()
     lax.fori_loop(0, 4, score_step, 0)
     send_lse(1)
@@ -188,15 +192,17 @@
     def places(slot):
         return (1, y, 2, z) if slot == 0 else (2, z, 1, y)
 
-    def send_a(i, slot):
+    def copies_a(i, slot):
         axis, p, _, _ = places(slot)
         up, down, far = lax.rem(p + 1, SIDE), lax.rem(p + 3, SIDE), lax.rem(p + 2, SIDE)
         to_up, to_down = along(axis, 1, 0), along(axis, 3, 0)
         lo, hi = pl.ds(0, 2), pl.ds(2, 2)
-        send(weighted.at[i, far, lo], gather_a.at[i, 0, 0], a_send, a_recv.at[i, 0], to_up)
-        send(weighted.at[i, far, hi], gather_a.at[i, 0, 1], a_send, a_recv.at[i, 0], to_down)
-        send(weighted.at[i, up, hi], gather_a.at[i, 1, 0], a_send, a_recv.at[i, 1], to_up)
-        send(weighted.at[i, down, lo], gather_a.at[i, 1, 1], a_send, a_recv.at[i, 1], to_down)
+        return [
+            (weighted.at[i, far, lo], gather_a.at[i, 0, 0], a_send, a_recv.at[i, 0], to_up),
+            (weighted.at[i, far, hi], gather_a.at[i, 0, 1], a_send, a_recv.at[i, 0], to_down),
+            (weighted.at[i, up, hi], gather_a.at[i, 1, 0], a_send, a_recv.at[i, 1], to_up),
+            (weighted.at[i, down, lo], gather_a.at[i, 1, 1], a_send, a_recv.at[i, 1], to_down),
+        ]
 
     def relay_sums(i, slot):
         _, p, _, _ = places(slot)
@@ -205,10 +211,12 @@
         relay[i, 0] = (weighted[i, up, 0:2].astype(F32) + gather_a[i, 0, 0].astype(F32)).astype(BF16)
         relay[i, 1] = (weighted[i, down, 2:4].astype(F32) + gather_a[i, 0, 1].astype(F32)).astype(BF16)
 
-    def send_b(i, slot):
+    def copies_b(i, slot):
         axis, _, _, _ = places(slot)
-        send(relay.at[i, 0], gather_b.at[i, 0], b_send, b_recv.at[i], along(axis, 1, 0))
-        send(relay.at[i, 1], gather_b.at[i, 1], b_send, b_recv.at[i], along(axis, 3, 0))
+        return [
+            (relay.at[i, 0], gather_b.at[i, 0], b_send, b_recv.at[i], along(axis, 1, 0)),
+            (relay.at[i, 1], gather_b.at[i, 1], b_send, b_recv.at[i], along(axis, 3, 0)),
+        ]
 
     def second_sums(i, slot):
         _, p, _, _ = places(slot)
@@ -219,13 +227,19 @@
         second[i, 0:2] = low.astype(BF16).reshape(2, 2, DEV_COLS, CHUNK)
         second[i, 2:4] = high.astype(BF16).reshape(2, 2, DEV_COLS, CHUNK)
 
-    def send_c(i, slot):
+    def copies_c(i, slot):
         _, _, axis, q = places(slot)
-        for j, (d, dc) in enumerate(OTHERS):
-            send(
-                second.at[i, lax.rem(q + d, SIDE), lax.rem(core + dc, 2)], gather_c.at[i, j],
-                c_send, c_recv.at[i], along(axis, d, dc),
-            )
+        copies = []
+        for j in FAR_FIRST:
+            d, dc = OTHERS[j]
+            part = second.at[i, lax.rem(q + d, SIDE), lax.rem(core + dc, 2)]
+            copies.append((part, gather_c.at[i, j], c_send, c_recv.at[i], along(axis, d, dc)))
+        return copies
+
+    def send_pair(copies, j):
+        for both in zip(copies(2 * j, 0), copies(2 * j + 1, 1)):
+            for copy in both:
+                send(*copy)
 
     def finish(i, slot):
         _, _, _, q = places(slot)
@@ -267,15 +281,15 @@
         exponentials(2 * j + 1, 1)
         product(2 * j + 1, 1)
         exponentials(jnp.minimum(2 * j + 2, N_CHUNKS - 1), 0)
-        send_a(2 * j, 0)
-        send_a(2 * j + 1, 1)
+        send_pair(copies_a, j)
         return carry
 
-    def pair(*steps):
+    def pair(step, copies=None):
         def both(j, carry):
-            for step in steps:
-                step(2 * j, 0)
-                step(2 * j + 1, 1)
+            step(2 * j, 0)
+            step(2 * j + 1, 1)
+            if copies is not None:
+                send_pair(copies, j)
             return carry
 
         lax.fori_loop(0, N_CHUNKS // 2, both, 0)
@@ -283,9 +297,9 @@
     exponentials(0, 0)
     lax.fori_loop(0, N_CHUNKS // 2, sums_step, 0)
     send_mass(0)
-    pair(relay_sums, send_b)
+    pair(relay_sums, copies_b)
     send_mass(1)
-    pair(second_sums, send_c)
+    pair(second_sums, copies_c)
     send_mass(2)
     pair(finish)
     wait(emb.at[pl.ds(ROWS, ROWS)], emb_send)
@@ -329,7 +343,7 @@
             pltpu.VMEM((16, 128), F32),
             pltpu.VMEM((7, 16, 128), F32),
             pltpu.VMEM((2, 16, 128), F32),
-            dma((3,)),
+            dma((4,)),
             dma, dma((2,)),
             dma, dma((2,)),
             dma, dma((N_CHUNKS, 2)),

time: 55.1 us -> 54.8 us (level)
  no operation moved by 1% of the time
where the time goes in v3:
time: 54.8 us; the launch traced here: 54.6 us
  Pallas kernels  51.1 us (93%)
  local copies, waits for them, and re-layouts  2.95 us (5%)
  between operations  0.64 us (1%)
    pallas_call x1, Pallas kernels, per_device(): pl.pallas_call(kernel, out_shape=(jax.ShapeDtypeStruct((8, 128), F32), ja...  51.1 us
    unnamed x2, local copies, waits for them, and re-layouts  2.95 us

profile of v3, /device:TPU:1, one launch (start us, length us, event | category | flops | bytes accessed | tf_op | source)
XLA Modules:
  0.0 54.6 jit_solution(10119021013614872724)
XLA Ops:
  0.6 51.1 %shard_map.41 = (f32[8,128]{1,0:T(8,128)}, bf16[32,4096]{1,0:T(8,128)(2,1)}) custom-call(bf16[1024,1024]{1,0:T(8,128)(2,1)} %e_hbm.1, bf16[4096,1024]{1,0:T(8,128)(2,1)} %c_hbm.1), custom_call_target="tpu_custom_call" | custom-call | tf_op jit(solution)/shard_map/pallas_call | solution.py:316
  51.7 1.3 %copy.6 = f32[1024]{0:T(1024)} copy(f32[1024]{0:T(1024)} %bitcast.3) | data formatting | bytes 8192
  53.0 1.7 %copy.7 = bf16[4096,32]{0,1:T(8,128)(2,1)} copy(bf16[4096,32]{0,1:T(8,128)(2,1)} %bitcast.2) | data formatting | bytes 524288

commit v4 on v3

--- a/solution.py
+++ b/solution.py
@@ -277,6 +277,12 @@
             den[1] = mass_in2[3] + mass_in2[4] + mass_in2[5] + mass_in2[6] + 1.0
 
     def sums_step(j, carry):
+        @pl.when(j == N_CHUNKS // 2 - 1)
+        def _():
+            relay_sums(0, 0)
+            relay_sums(1, 1)
+            send_pair(copies_b, 0)
+
         product(2 * j, 0)
         exponentials(2 * j + 1, 1)
         product(2 * j + 1, 1)
@@ -284,7 +290,7 @@
         send_pair(copies_a, j)
         return carry
 
-    def pair(step, copies=None):
+    def pair(step, copies=None, first=0):
         def both(j, carry):
             step(2 * j, 0)
             step(2 * j + 1, 1)
@@ -292,12 +298,12 @@
                 send_pair(copies, j)
             return carry
 
-        lax.fori_loop(0, N_CHUNKS // 2, both, 0)
+        lax.fori_loop(first, N_CHUNKS // 2, both, 0)
 
     exponentials(0, 0)
     lax.fori_loop(0, N_CHUNKS // 2, sums_step, 0)
     send_mass(0)
-    pair(relay_sums, copies_b)
+    pair(relay_sums, copies_b, 1)
     send_mass(1)
     pair(second_sums, copies_c)
     send_mass(2)

time: 54.8 us -> 54.8 us (level)
  no operation moved by 1% of the time
where the time goes in v4:
time: 54.8 us; the launch traced here: 54.7 us
  Pallas kernels  51.1 us (93%)
  local copies, waits for them, and re-layouts  2.95 us (5%)
  between operations  0.64 us (1%)
    pallas_call x1, Pallas kernels, per_device(): pl.pallas_call(kernel, out_shape=(jax.ShapeDtypeStruct((8, 128), F32), ja...  51.1 us
    unnamed x2, local copies, waits for them, and re-layouts  2.95 us

profile of v4, /device:TPU:1, one launch (start us, length us, event | category | flops | bytes accessed | tf_op | source)
XLA Modules:
  0.0 54.7 jit_solution(772382873707122130)
XLA Ops:
  0.6 51.1 %shard_map.41 = (f32[8,128]{1,0:T(8,128)}, bf16[32,4096]{1,0:T(8,128)(2,1)}) custom-call(bf16[1024,1024]{1,0:T(8,128)(2,1)} %e_hbm.1, bf16[4096,1024]{1,0:T(8,128)(2,1)} %c_hbm.1), custom_call_target="tpu_custom_call" | custom-call | tf_op jit(solution)/shard_map/pallas_call | solution.py:322
  51.7 1.3 %copy.6 = f32[1024]{0:T(1024)} copy(f32[1024]{0:T(1024)} %bitcast.3) | data formatting | bytes 8192
  53.0 1.7 %copy.7 = bf16[4096,32]{0,1:T(8,128)(2,1)} copy(bf16[4096,32]{0,1:T(8,128)(2,1)} %bitcast.2) | data formatting | bytes 524288
